TPU v7x, 32 devices: a whole 2x2x4 slice. The times are simulated.
32 devices in a mesh: replica: 4 (over x, core), fsdp: 8 (over z, y).
Axes of the slice: x: 2, y: 2, z: 4, core: 2. Of those that a mesh axis runs over, the one named last changes fastest.
Arguments:
- hidden_in: bfloat16 [4096, 4096], P(('replica', 'fsdp')), may hold values from -60 to 60
- res_grad: bfloat16 [4096, 4096], P(('replica', 'fsdp')), may hold values from -0.59765625 to 0.59765625
- value_grad: bfloat16 [4096, 512], P(('replica', 'fsdp')), may hold values from -1.5 to 1.5
- value_weight: bfloat16 [4, 4096, 512], P('replica', 'fsdp'), may hold values from -0.09375 to 0.09375
- norm_gain: float32 [4, 4096], P('replica'), may hold values from 0.5 to 1.5
- inner_frag: float32 [4, 4096, 768], P('replica', 'fsdp'), may hold values from -6 to 6
- outer_frag: float32 [4096, 768], P('fsdp'), may hold values from -6 to 6
- momentum: float32 [4096, 768], P('fsdp'), may hold values from -3 to 3
Outputs:
- hidden_grad: bfloat16 [4096, 4096], P(('replica', 'fsdp'))
- weight_grad: bfloat16 [4, 4096, 512], P('replica', 'fsdp')
- gain_grad: float32 [4, 4096], P('replica', 'fsdp')
- new_outer: float32 [4096, 768], P('fsdp')
- new_momentum: float32 [4096, 768], P('fsdp')
All inputs are finite; a program needn't handle non-finite values.
Results may differ from a plain program's by a relative error of at most 0.015.
Values may be sent and summed in bfloat16 or wider, within the bound.
A program may use at most 64 MiB of HBM per device.

v0:
```python
import jax
import jax.numpy as jnp
from jax import lax
from jax.sharding import PartitionSpec as P


def body(
    hidden_in, res_grad, value_grad, value_weight, norm_gain, inner_frag, outer_frag, momentum
):
    pseudo_grad = outer_frag - inner_frag[0]
    average = lax.psum_scatter(
        pseudo_grad, "replica", scatter_dimension=1, tiled=True
    ) / lax.axis_size("replica")
    share_width = average.shape[1]
    offset = lax.axis_index("replica") * share_width
    old_momentum = lax.dynamic_slice_in_dim(momentum, offset, share_width, 1)
    old_outer = lax.dynamic_slice_in_dim(outer_frag, offset, share_width, 1)
    momentum_share = 0.9 * old_momentum + average
    outer_share = old_outer - 0.7 * (average + 0.9 * momentum_share)
    new_outer, new_momentum = (
        lax.all_gather(outer_share.astype(jnp.bfloat16), "replica", axis=1, tiled=True).astype(
            outer_share.dtype
        ),
        lax.all_gather(momentum_share.astype(jnp.bfloat16), "replica", axis=1, tiled=True).astype(
            momentum_share.dtype
        ),
    )
    widened = hidden_in.astype(jnp.float32)
    inverse = lax.rsqrt(jnp.mean(widened * widened, axis=1, keepdims=True) + 1e-05)
    unit_rows = widened * inverse
    scales = norm_gain[0]
    normed = (unit_rows * scales).astype(jnp.bfloat16)
    input_grad = lax.dot_general(
        value_grad,
        lax.all_gather(value_weight[0], "fsdp", axis=0, tiled=True),
        (((1,), (1,)), ((), ())),
        preferred_element_type=jnp.float32,
    )
    partial_gain = jnp.sum(input_grad * unit_rows, axis=0)
    row_share = value_weight.shape[1]
    gain_sum = lax.psum(partial_gain, "fsdp")
    gain_grad = lax.dynamic_slice_in_dim(gain_sum, lax.axis_index("fsdp") * row_share, row_share, 0)
    scaled = input_grad * scales
    projection = jnp.mean(scaled * unit_rows, axis=1, keepdims=True)
    hidden_grad = (
        res_grad.astype(jnp.float32) + inverse * (scaled - unit_rows * projection)
    ).astype(jnp.bfloat16)
    weight_grad = lax.psum_scatter(
        lax.dot_general(
            normed, value_grad, (((0,), (0,)), ((), ())), preferred_element_type=jnp.float32
        ).astype(jnp.bfloat16),
        "fsdp",
        scatter_dimension=0,
        tiled=True,
    )
    return (hidden_grad, weight_grad[None], gain_grad[None], new_outer, new_momentum)


def solution(mesh):
    in_specs = (
        P(("replica", "fsdp"), None),
        P(("replica", "fsdp"), None),
        P(("replica", "fsdp"), None),
        P("replica", "fsdp", None),
        P("replica", None),
        P("replica", "fsdp", None),
        P("fsdp", None),
        P("fsdp", None),
    )
    out_specs = (
        P(("replica", "fsdp"), None),
        P("replica", "fsdp", None),
        P("replica", "fsdp"),
        P("fsdp", None),
        P("fsdp", None),
    )
    return jax.shard_map(body, mesh=mesh, in_specs=in_specs, out_specs=out_specs, check_vma=False)
```

profile of v0, /device:TPU:0, one launch (start us, length us, event | category | flops | bytes accessed | tf_op | source)
XLA Modules:
  0.0 173.9 jit_solution(1429464102791935696)
XLA Ops:
  8.0 0.0 copy-start
  8.0 0.0 reduce-scatter.7.cloned.1.call-start
  8.1 2.1 %bitcast_subtract_fusion = f32[512,768]{1,0:T(8,128)S(1)} fusion(f32[512,768]{1,0:T(8,128)} %param.14, f32[1,512,768]{2,1,0:T(8,128)} %param.13), kind=kLoop, calls=%fused_computation.17 | loop fusion | flops 393216 | bytes 4718592 | tf_op jit(solution)/shard_map/sub | solution.py:10
  10.2 0.0 copy-start.1
  10.2 1.6 copy.22
  11.8 0.0 copy-start.2
  11.8 0.0 reduce-scatter.7.cloned.1.call-update
  11.8 0.0 all-gather.3.cloned.1.call-start
  11.9 0.5 all-gather.3.cloned.1.call-update
  12.4 0.0 reduce-scatter.5.cloned.1.call-start
  12.4 0.0 copy-done.1
  12.5 0.3 fusion.13
  12.7 0.0 copy-done
  12.8 0.0 copy-done.2
  12.8 3.3 %convolution_convert_fusion = bf16[4096,512]{1,0:T(8,128)(2,1)} fusion(bf16[128,512]{1,0:T(8,128)(2,1)S(1)} %copy-done, bf16[128,4096]{1,0:T(8,128)(2,1)S(1)} %copy-done.1, f32[4096]{0:T(1024)S(1)} %bitcast.24, f32[128]{0:T(128)S(1)} %add_rsqrt_fusion), kind=kOutput, calls=%fused_computation | convolution fusion | flops 541065216 | bytes 5390848 | tf_op jit(solution)/shard_map/dot_general | solution.py:49
  16.1 0.0 reduce-scatter.5.cloned.1.call-update
  16.1 1.7 constant_dynamic-slice_fusion
  17.9 0.2 copy.25
  18.0 0.2 copy.24
  18.2 24.7 %reduce-scatter.7.cloned.1.call-done = f32[192,512]{1,0:T(8,128)} async-done(((f32[768,512]{1,0:T(8,128)}), f32[192,512]{1,0:T(8,128)}) %reduce-scatter.7.cloned.1.call-update) | async-done | bytes 393232
  42.9 1.1 fusion.17
  44.0 8.2 %all_gather.10 = bf16[512,768]{0,1:T(8,128)(2,1)S(1)} all-gather(bf16[512,192]{0,1:T(8,128)(2,1)S(1)} %get-tuple-element.18), channel_id=1, replica_groups=mesh['replica'=4,'fsdp'=8] {'replica'}, dimensions={1}, use_global_device_ids=true | all-gather | bytes 983040 | tf_op jit(solution)/shard_map/all_gather | solution.py:21
  52.2 1.4 copy.20
  53.6 8.7 %all_gather.11 = bf16[512,768]{0,1:T(8,128)(2,1)S(1)} all-gather(bf16[512,192]{0,1:T(8,128)(2,1)S(1)} %get-tuple-element.17), channel_id=1, replica_groups=mesh['replica'=4,'fsdp'=8] {'replica'}, dimensions={1}, use_global_device_ids=true | all-gather | bytes 983040 | tf_op jit(solution)/shard_map/all_gather | solution.py:24
  62.4 1.4 copy.21
  63.8 35.3 %all-gather.3.cloned.1.call-done = bf16[1,4096,512]{2,1,0:T(8,128)(2,1)} async-done(((bf16[1,512,512]{2,1,0:T(8,128)(2,1)}), bf16[1,4096,512]{2,1,0:T(8,128)(2,1)}) %all-gather.3.cloned.1.call-update) | async-done | bytes 4194320 | tf_op jit(solution)/shard_map/all_gather | solution.py:35
  99.1 3.8 %fusion.12 = (f32[4096]{0:T(1024)S(1)}, f32[128]{0:T(128)S(1)}, f32[128,4096]{1,0:T(8,128)S(1)}) fusion(bf16[128,4096]{1,0:T(8,128)(2,1)S(1)} %copy-done.1, f32[128]{0:T(128)S(1)} %add_rsqrt_fusion, f32[4096]{0:T(1024)S(1)} %bitcast.25, bf16[128,512]{1,0:T(8,128)(2,1)S(1)} %copy-done, bf16[1,4096,512]{2,1,0:T(8,128)(2,1)} %all-gather.3.cloned.1.call-done), kind=kOutput, calls=%fused_computation.15 | convolution fusion | flops 540536704 | bytes 7504896 | tf_op jit(solution)/shard_map/dot_general | solution.py:33
  102.9 36.7 %psum.7 = f32[4096]{0:T(1024)S(1)} all-reduce(f32[4096]{0:T(1024)S(1)} %get-tuple-element.15), channel_id=1, replica_groups=mesh['replica'=4,'fsdp'=8] {'fsdp'}, use_global_device_ids=true, to_apply=%region_4.0 | all-reduce | flops 4096 | bytes 32768 | tf_op jit(solution)/shard_map/psum | solution.py:41
  139.6 0.7 dynamic_slice.9
  140.2 2.9 %fusion.10 = bf16[128,4096]{1,0:T(8,128)(2,1)} fusion(bf16[128,4096]{1,0:T(8,128)(2,1)S(1)} %copy-done.1, bf16[128,4096]{1,0:T(8,128)(2,1)} %param.9, f32[128,4096]{1,0:T(8,128)S(1)} %get-tuple-element.19, f32[128]{0:T(128)S(1)} %broadcast_multiply_fusion, f32[4096]{0:T(1024)S(1)} %bitcast.26, f32[128]{0:T(128)S(1)} %add_rsqrt_fusion), kind=kLoop, calls=%fused_computation.13 | loop fusion | flops 4718592 | bytes 5260288 | tf_op jit(solution)/shard_map/convert_element_type | solution.py:47
  143.1 23.3 %reduce-scatter.5.cloned.1.call-done = bf16[512,512]{1,0:T(8,128)(2,1)} async-done(((bf16[4096,512]{1,0:T(8,128)(2,1)}), bf16[512,512]{1,0:T(8,128)(2,1)}) %reduce-scatter.5.cloned.1.call-update) | async-done | bytes 524304 | tf_op jit(solution)/shard_map/reduce_scatter | solution.py:48
  (2 shorter events, 0.0 us)
Async XLA Ops:
  8.0 4.8 %copy-start = (bf16[128,512]{1,0:T(8,128)(2,1)S(1)}, bf16[128,512]{1,0:T(8,128)(2,1)}, u32[]{:S(2)}) copy-start(bf16[128,512]{1,0:T(8,128)(2,1)} %param.10) | copy-start | bytes 393220
  8.0 34.9 %reduce-scatter.7.cloned.1.call-start = ((), (), s32[]{:S(2)}) async-start(), calls=%async_computation.4 | async-start | bytes 1966080
  10.2 2.3 %copy-start.1 = (bf16[128,4096]{1,0:T(8,128)(2,1)S(1)}, bf16[128,4096]{1,0:T(8,128)(2,1)}, u32[]{:S(2)}) copy-start(bf16[128,4096]{1,0:T(8,128)(2,1)} %param.8) | copy-start | bytes 3145732
  11.8 1.0 copy-start.2
  11.8 87.2 %all-gather.3.cloned.1.call-start = ((), (), s32[]{:S(2)}) async-start(), calls=%async_computation.3 | async-start | bytes 4718592 | tf_op jit(solution)/shard_map/all_gather | solution.py:35
  12.4 154.0 %reduce-scatter.5.cloned.1.call-start = ((), (), s32[]{:S(2)}) async-start(), calls=%async_computation.2 | async-start | bytes 4718592 | tf_op jit(solution)/shard_map/reduce_scatter | solution.py:48
Sparse Core Ops, SparseCore 0:
  12.0 30.8 reduce-scatter.6
  47.5 118.8 reduce-scatter.4
Sparse Core Ops, SparseCore 1:
  14.4 84.6 all-gather.2
where the time goes:
time: 174 us
  waiting for transfers between devices  83.8 us (48%)
  blocking collectives  53.6 us (31%)
  between operations  15.6 us (9%)
  local copies, waits for them, and re-layouts  7.19 us (4%)
  matrix products  7.14 us (4%)
  other arithmetic  6.4 us (4%)
    psum x1, blocking collectives, body(): gain_sum = lax.psum(partial_gain, 'fsdp')  36.7 us
    all_gather x1, waiting for transfers between devices, body(): lax.all_gather(value_weight[0], 'fsdp', axis=0, tiled=True)  35.3 us
    unnamed x4, waiting for transfers between devices  25.2 us
    reduce_scatter x1, waiting for transfers between devices, body(): lax.psum_scatter(lax.dot_general(normed, value_grad, (((0,), (0,)), ((),...  23.3 us
    all_gather x1, blocking collectives, body(): lax.all_gather(momentum_share.astype(jnp.bfloat16), 'replica', axis=1, ti...  8.7 us
    all_gather x1, blocking collectives, body(): lax.all_gather(outer_share.astype(jnp.bfloat16), 'replica', axis=1, tiled...  8.21 us
    unnamed x11, local copies, waits for them, and re-layouts  4.83 us
    dot_general x1, matrix products, body(): lax.dot_general(value_grad, lax.all_gather(value_weight[0], 'fsdp', axis=...  3.79 us
  transfers between devices with their start and end apart: 3, of which 3 were waited for; matrix products, arithmetic and copies ran while one was open for 10% of the time, Pallas kernels for 0%

commit v1 on v0

v1 whole, which is shorter than its diff:
```python
import functools

import jax
import jax.numpy as jnp
from jax import lax
from jax.experimental import pallas as pl
from jax.experimental.pallas import tpu as pltpu
from jax.sharding import PartitionSpec as P

MESH = pl.DeviceIdType.MESH
F32 = jnp.float32
BF16 = jnp.bfloat16
EPS = 1e-05


def kernel(
    n, reps, with_frag,
    hid, res_h, vg, w, gain, inner_h, outer_h, mom_h,
    hg_h, wg_out, gg_out, no_h, nm_h,
    inv, nrm_s, nrm_r, vg_r, ig_s, ig_r, wg_acc, res, hg,
    inner, outer, mom, ps, fr_r, av,
    vg_send, vg_recv, nrm_send, nrm_recv, ig_send, ig_recv,
    fr_send, fr_recv, av_send, av_recv, local,
):
    tokens, width = hid.shape
    feats = width // n
    half = n // 2
    me = lax.axis_index("fsdp")
    rep = lax.axis_index("replica")
    zrow, ycol = me // 2, lax.rem(me, 2)
    mirror = (half - 1 - zrow) * 2 + ycol
    base = (me // half) * half
    far = half - base
    mine, theirs = me - base, mirror - far

    def near_peer(j):
        return base + lax.rem(mine + j, half)

    def far_peer(j):
        return far + lax.rem(theirs + j, half)

    def cols(i):
        return pl.ds(pl.multiple_of(i * feats, feats), feats)

    def remote(src, dst, send, recv, dest, axis="fsdp"):
        return pltpu.make_async_remote_copy(
            src_ref=src, dst_ref=dst, send_sem=send, recv_sem=recv,
            device_id={axis: dest}, device_id_type=MESH,
        )

    loads = [pltpu.make_async_copy(res_h, res, local.at[0])]
    if with_frag:
        loads += [
            pltpu.make_async_copy(inner_h, inner, local.at[1]),
            pltpu.make_async_copy(outer_h, outer, local.at[2]),
            pltpu.make_async_copy(mom_h, mom, local.at[3]),
        ]
    for load in loads:
        load.start()

    barrier = pltpu.get_barrier_semaphore()
    for k in range(1, n):
        pl.semaphore_signal(
            barrier, inc=1, device_id={"fsdp": lax.rem(me + k, n)}, device_id_type=MESH
        )
    if with_frag:
        for k in range(1, reps):
            pl.semaphore_signal(
                barrier, inc=1, device_id={"replica": lax.rem(rep + k, reps)}, device_id_type=MESH
            )
    pl.semaphore_wait(barrier, n - 1 + (reps - 1 if with_frag else 0))

    def vg_own(slot, dest):
        return remote(vg, vg_r.at[me], vg_send.at[slot], vg_recv.at[me], dest)

    def vg_forward(j):
        return remote(
            vg_r.at[mirror], vg_r.at[mirror], vg_send.at[half + j], vg_recv.at[mirror], near_peer(j)
        )

    vg_own(0, mirror).start()
    for j in range(1, half):
        vg_own(j, near_peer(j)).start()
    vg_r[me] = vg[...]

    rows = 16

    @pl.loop(0, tokens // rows)
    def _(c):
        at = pl.ds(pl.multiple_of(c * rows, rows), rows)
        total = jnp.zeros((rows, feats), F32)
        for b in range(n):
            x = hid[at, b * feats:(b + 1) * feats].astype(F32)
            total += x * x
        mean = jnp.sum(total, axis=1, keepdims=True) / width
        inv[at, :] = jnp.broadcast_to(lax.rsqrt(mean + EPS), (rows, 128))

    def norm_block(dest, out, slot):
        scale = gain[:, cols(dest)]

        @pl.loop(0, tokens // rows)
        def _(c):
            at = pl.ds(pl.multiple_of(c * rows, rows), rows)
            unit = hid[at, cols(dest)].astype(F32) * inv[at, 0:1]
            out[slot, at, :] = (unit * scale).astype(BF16)

    def nrm_copy(dest):
        return remote(
            nrm_s.at[dest], nrm_r.at[me], nrm_send.at[dest], nrm_recv.at[me], dest
        )

    @pl.loop(0, half)
    def _(j):
        dest = far_peer(j)
        norm_block(dest, nrm_s, dest)
        nrm_copy(dest).start()

    @pl.loop(1, half)
    def _(j):
        dest = near_peer(j)
        norm_block(dest, nrm_s, dest)
        nrm_copy(dest).start()

    norm_block(me, nrm_r, me)

    def fr_copy(k):
        dest = lax.rem(rep + k, reps)
        return remote(
            ps.at[dest], fr_r.at[rep], fr_send.at[dest], fr_recv.at[rep], dest, "replica"
        )

    def av_copy(k):
        dest = lax.rem(rep + k, reps)
        return remote(
            av.at[rep], av.at[rep], av_send.at[dest], av_recv.at[rep], dest, "replica"
        )

    if with_frag:
        share = ps.shape[1]
        steps = share // rows
        for load in loads[1:]:
            load.wait()

        @pl.loop(0, reps * steps)
        def _(c):
            at = pl.ds(pl.multiple_of(c * rows, rows), rows)
            to = pl.ds(pl.multiple_of(lax.rem(c, steps) * rows, rows), rows)
            ps[c // steps, to, :] = (outer[at, :] - inner[at, :]).astype(BF16)

        for k in range(1, reps):
            fr_copy(k).start()

    remote(vg, vg_r.at[mirror], vg_send.at[0], vg_recv.at[mirror], mirror).wait_recv()
    for j in range(1, half):
        vg_forward(j).start()

    def ig_dot(src):
        return lax.dot_general(
            vg_r[src], w[...], (((1,), (1,)), ((), ())), preferred_element_type=F32
        ).astype(BF16)

    def ig_copy(src):
        return remote(ig_s.at[src], ig_r.at[me], ig_send.at[src], ig_recv.at[me], src)

    def vg_wait(src):
        remote(vg, vg_r.at[src], vg_send.at[0], vg_recv.at[src], src).wait_recv()

    ig_s[mirror] = ig_dot(mirror)
    ig_copy(mirror).start()

    @pl.loop(1, half)
    def _(j):
        src = near_peer(j)
        vg_wait(src)
        ig_s[src] = ig_dot(src)
        ig_copy(src).start()

    @pl.loop(1, half)
    def _(j):
        src = far_peer(j)
        vg_wait(src)
        ig_s[src] = ig_dot(src)
        ig_copy(src).start()

    own = ig_dot(me)
    ig_s[me] = own
    ig_r[me] = own

    stores = []
    if with_frag:
        for k in range(1, reps):
            src = lax.rem(rep + k, reps)
            remote(
                ps.at[src], fr_r.at[src], fr_send.at[src], fr_recv.at[src], src, "replica"
            ).wait_recv()
        fr_r[rep] = ps[rep]

        @pl.loop(0, steps)
        def _(c):
            at = pl.ds(pl.multiple_of(c * rows, rows), rows)
            total = fr_r[0, at, :].astype(F32)
            for r in range(1, reps):
                total += fr_r[r, at, :].astype(F32)
            av[rep, at, :] = (total / reps).astype(BF16)

        for k in range(1, reps):
            av_copy(k).start()
        for k in range(1, reps):
            src = lax.rem(rep + k, reps)
            remote(
                av.at[src], av.at[src], av_send.at[src], av_recv.at[src], src, "replica"
            ).wait_recv()

        @pl.loop(0, reps * steps)
        def _(c):
            at = pl.ds(pl.multiple_of(c * rows, rows), rows)
            to = pl.ds(pl.multiple_of(lax.rem(c, steps) * rows, rows), rows)
            average = av[c // steps, to, :].astype(F32)
            momentum = 0.9 * mom[at, :] + average
            mom[at, :] = momentum
            outer[at, :] = outer[at, :] - 0.7 * (average + 0.9 * momentum)

        stores += [
            pltpu.make_async_copy(outer, no_h, local.at[1]),
            pltpu.make_async_copy(mom, nm_h, local.at[2]),
        ]
        for store in stores:
            store.start()

    loads[0].wait()

    @pl.loop(1, n)
    def _(k):
        src = lax.rem(me + k, n)
        remote(ig_s.at[src], ig_r.at[src], ig_send.at[src], ig_recv.at[src], src).wait_recv()

    @pl.loop(0, tokens // rows)
    def _(c):
        at = pl.ds(pl.multiple_of(c * rows, rows), rows)
        inverse = inv[at, 0:1]
        total = jnp.zeros((rows, feats), F32)
        for b in range(n):
            span = slice(b * feats, (b + 1) * feats)
            unit = hid[at, span].astype(F32) * inverse
            total += (ig_r[b, at, :].astype(F32) * gain[:, span]) * unit
        projection = jnp.sum(total, axis=1, keepdims=True) / width
        for b in range(n):
            span = slice(b * feats, (b + 1) * feats)
            unit = hid[at, span].astype(F32) * inverse
            scaled = ig_r[b, at, :].astype(F32) * gain[:, span]
            hg[at, span] = (
                res[at, span].astype(F32) + inverse * (scaled - unit * projection)
            ).astype(BF16)

    store = pltpu.make_async_copy(hg, hg_h, local.at[0])
    store.start()
    stores.append(store)

    def wg_dot(src):
        return lax.dot_general(
            nrm_r[src], vg_r[src], (((0,), (0,)), ((), ())), preferred_element_type=F32
        )

    def gg_sum(src):
        return jnp.sum(nrm_r[src].astype(F32) * ig_s[src].astype(F32), axis=0, keepdims=True)

    wg_acc[...] = wg_dot(me)
    gg_out[...] = gg_sum(me)

    @pl.loop(1, n)
    def _(k):
        src = lax.rem(me + k, n)
        remote(
            nrm_s.at[src], nrm_r.at[src], nrm_send.at[src], nrm_recv.at[src], src
        ).wait_recv()
        wg_acc[...] += wg_dot(src)
        gg_out[...] += gg_sum(src)

    wg_out[...] = wg_acc[...].astype(BF16)
    gg_out[...] = gg_out[...] / gain[:, cols(me)]

    vg_own(0, mirror).wait_send()
    for j in range(1, half):
        vg_own(j, near_peer(j)).wait_send()
        vg_forward(j).wait_send()
    for k in range(1, n):
        nrm_copy(lax.rem(me + k, n)).wait_send()
        ig_copy(lax.rem(me + k, n)).wait_send()
    if with_frag:
        for k in range(1, reps):
            fr_copy(k).wait_send()
            av_copy(k).wait_send()
    for store in stores:
        store.wait()


def outer_step(inner_frag, outer_frag, momentum):
    pseudo_grad = outer_frag - inner_frag
    average = lax.psum_scatter(
        pseudo_grad, "replica", scatter_dimension=1, tiled=True
    ) / lax.axis_size("replica")
    average = lax.all_gather(average.astype(BF16), "replica", axis=1, tiled=True).astype(F32)
    new_momentum = 0.9 * momentum + average
    return outer_frag - 0.7 * (average + 0.9 * new_momentum), new_momentum


def body(
    hidden_in, res_grad, value_grad, value_weight, norm_gain, inner_frag, outer_frag, momentum
):
    n, reps = lax.axis_size("fsdp"), lax.axis_size("replica")
    tokens, width = hidden_in.shape
    values = value_grad.shape[1]
    feats = value_weight.shape[1]
    frag_rows, frag_cols = outer_frag.shape
    with_frag = frag_rows % (16 * reps) == 0
    share = frag_rows // reps if with_frag else 16
    slots = reps if with_frag else 1
    frag_buffer = (frag_rows, frag_cols) if with_frag else (8, 128)
    half_buffer = (slots, share, frag_cols) if with_frag else (1, 16, 128)

    vmem = pl.BlockSpec(memory_space=pltpu.VMEM)
    anywhere = pl.BlockSpec(memory_space=pl.ANY)
    frag_out = frag_buffer
    dma = pltpu.SemaphoreType.DMA
    hidden_grad, weight_grad, gain_grad, new_outer, new_momentum = pl.pallas_call(
        functools.partial(kernel, n, reps, with_frag),
        out_shape=(
            jax.ShapeDtypeStruct((tokens, width), BF16),
            jax.ShapeDtypeStruct((feats, values), BF16),
            jax.ShapeDtypeStruct((1, feats), F32),
            jax.ShapeDtypeStruct(frag_out, F32),
            jax.ShapeDtypeStruct(frag_out, F32),
        ),
        in_specs=[vmem, anywhere, vmem, vmem, vmem, anywhere, anywhere, anywhere],
        out_specs=(anywhere, vmem, vmem, anywhere, anywhere),
        scratch_shapes=[
            pltpu.VMEM((tokens, 128), F32),
            pltpu.VMEM((n, tokens, feats), BF16),
            pltpu.VMEM((n, tokens, feats), BF16),
            pltpu.VMEM((n, tokens, values), BF16),
            pltpu.VMEM((n, tokens, feats), BF16),
            pltpu.VMEM((n, tokens, feats), BF16),
            pltpu.VMEM((feats, values), F32),
            pltpu.VMEM((tokens, width), BF16),
            pltpu.VMEM((tokens, width), BF16),
            pltpu.VMEM(frag_buffer, F32),
            pltpu.VMEM(frag_buffer, F32),
            pltpu.VMEM(frag_buffer, F32),
            pltpu.VMEM(half_buffer, BF16),
            pltpu.VMEM(half_buffer, BF16),
            pltpu.VMEM(half_buffer, BF16),
            dma((n,)), dma((n,)), dma((n,)), dma((n,)), dma((n,)), dma((n,)),
            dma((slots,)), dma((slots,)), dma((slots,)), dma((slots,)), dma((4,)),
        ],
        compiler_params=pltpu.CompilerParams(
            collective_id=0, has_side_effects=True, vmem_limit_bytes=40 * 2**20
        ),
    )(
        hidden_in, res_grad, value_grad, value_weight[0], norm_gain,
        inner_frag[0], outer_frag, momentum,
    )
    if not with_frag:
        new_outer, new_momentum = outer_step(inner_frag[0], outer_frag, momentum)
    return (hidden_grad, weight_grad[None], gain_grad, new_outer, new_momentum)


def solution(mesh):
    in_specs = (
        P(("replica", "fsdp"), None),
        P(("replica", "fsdp"), None),
        P(("replica", "fsdp"), None),
        P("replica", "fsdp", None),
        P("replica", None),
        P("replica", "fsdp", None),
        P("fsdp", None),
        P("fsdp", None),
    )
    out_specs = (
        P(("replica", "fsdp"), None),
        P("replica", "fsdp", None),
        P("replica", "fsdp"),
        P("fsdp", None),
        P("fsdp", None),
    )
    return jax.shard_map(body, mesh=mesh, in_specs=in_specs, out_specs=out_specs, check_vma=False)
```

time: 174 us -> 78.3 us (0.45)
  waiting for transfers between devices: 83.8 us -> 0 us
  Pallas kernels: 0 us -> 62.9 us
  blocking collectives: 53.6 us -> 0 us
  between operations: 15.6 us -> 0.66 us
  matrix products: 7.14 us -> 0 us
  local copies, waits for them, and re-layouts: 7.19 us -> 14 us
  other arithmetic: 6.4 us -> 0 us
    pallas_call x0 -> x1, Pallas kernels: none -> 62.9 us  [body(): pl.pallas_call(functools.partial(kernel, n, reps, with_frag), out_shape=(...]
    psum x1 -> x0, blocking collectives: 36.7 us -> none  [body(): gain_sum = lax.psum(partial_gain, 'fsdp')]
    all_gather x1 -> x0, waiting for transfers between devices: 35.3 us -> none  [body(): lax.all_gather(value_weight[0], 'fsdp', axis=0, tiled=True)]
    unnamed x4 -> x0, waiting for transfers between devices: 25.2 us -> none
    reduce_scatter x1 -> x0, waiting for transfers between devices: 23.3 us -> none  [body(): lax.psum_scatter(lax.dot_general(normed, value_grad, (((0,), (0,)), ((),...]
    all_gather x2 -> x0, blocking collectives: 16.9 us -> none  [the longest x1 8.7 us: body(): lax.all_gather(momentum_share.astype(jnp.bfloat16), 'replica', axis=1, ti...]
    unnamed x11 -> x21, local copies, waits for them, and re-layouts: 4.83 us -> 14 us
    dot_general x2 -> x0, matrix products: 7.14 us -> none  [the longest x1 3.79 us: body(): lax.dot_general(value_grad, lax.all_gather(value_weight[0], 'fsdp', axis=...]
  transfers between devices with their start and end apart: 3 -> 0, of which waited for: 3 -> 0; matrix products, arithmetic and copies ran while one was open for 10% -> 0% of each run, Pallas kernels for 0% -> 0%
where the time goes in v1:
time: 78.3 us; the launch traced here: 77.5 us
  Pallas kernels  62.9 us (80%)
  local copies, waits for them, and re-layouts  14 us (18%)
    pallas_call x1, Pallas kernels, body(): pl.pallas_call(functools.partial(kernel, n, reps, with_frag), out_shape=(...  62.9 us
    unnamed x21, local copies, waits for them, and re-layouts  14 us

profile of v1, /device:TPU:0, one launch (start us, length us, event | category | flops | bytes accessed | tf_op | source)
XLA Modules:
  0.0 77.5 jit_solution(18376538774465942693)
XLA Ops:
  0.6 0.0 copy-start
  0.6 1.4 %copy-done = f32[1,512,768]{2,1,0:T(8,128)S(1)} copy-done((f32[1,512,768]{2,1,0:T(8,128)S(1)}, f32[1,512,768]{2,1,0:T(8,128)}, u32[]{:S(2)}) %copy-start) | copy-done | bytes 1572888
  2.0 0.0 copy-start.1
  2.0 1.4 %copy-done.1 = f32[512,768]{1,0:T(8,128)S(1)} copy-done((f32[512,768]{1,0:T(8,128)S(1)}, f32[512,768]{1,0:T(8,128)}, u32[]{:S(2)}) %copy-start.1) | copy-done | bytes 1572888
  3.5 0.0 copy-start.2
  3.5 1.4 %copy-done.2 = f32[512,768]{1,0:T(8,128)S(1)} copy-done((f32[512,768]{1,0:T(8,128)S(1)}, f32[512,768]{1,0:T(8,128)}, u32[]{:S(2)}) %copy-start.2) | copy-done | bytes 1572888
  4.9 0.0 copy-start.3
  4.9 1.2 %copy-done.3 = bf16[128,4096]{1,0:T(8,128)(2,1)S(1)} copy-done((bf16[128,4096]{1,0:T(8,128)(2,1)S(1)}, bf16[128,4096]{1,0:T(8,128)(2,1)}, u32[]{:S(2)}) %copy-start.3) | copy-done | bytes 1048600
  6.1 0.0 copy-start.4
  6.1 1.2 %copy-done.4 = bf16[128,4096]{1,0:T(8,128)(2,1)S(1)} copy-done((bf16[128,4096]{1,0:T(8,128)(2,1)S(1)}, bf16[128,4096]{1,0:T(8,128)(2,1)}, u32[]{:S(2)}) %copy-start.4) | copy-done | bytes 1048600
  7.3 0.0 copy-start.5
  7.3 1.0 %copy-done.5 = bf16[1,512,512]{2,1,0:T(8,128)(2,1)S(1)} copy-done((bf16[1,512,512]{2,1,0:T(8,128)(2,1)S(1)}, bf16[1,512,512]{2,1,0:T(8,128)(2,1)}, u32[]{:S(2)}) %copy-start.5) | copy-done | bytes 524312
  8.4 0.0 copy-start.6
  8.4 0.9 %copy-done.6 = bf16[128,512]{1,0:T(8,128)(2,1)S(1)} copy-done((bf16[128,512]{1,0:T(8,128)(2,1)S(1)}, bf16[128,512]{1,0:T(8,128)(2,1)}, u32[]{:S(2)}) %copy-start.6) | copy-done | bytes 131096
  9.3 0.0 copy-start.7
  9.3 0.7 copy-done.7
  10.0 62.9 %shard_map.119 = (bf16[128,4096]{1,0:T(8,128)(2,1)S(1)}, bf16[512,512]{1,0:T(8,128)(2,1)S(1)}, f32[1,512]{1,0:T(1,128)S(1)}, f32[512,768]{1,0:T(8,128)S(1)}, f32[512,768]{1,0:T(8,128)S(1)}) custom-call(bf16[128,4096]{1,0:T(8,128)(2,1)S(1)} %copy-done.3, bf16[128,4096]{1,0:T(8,128)(2,1)S(1)} %copy-done.4, bf16[128,512]{1,0:T(8,128)(2,1)S(1)} %copy-done.6, ...), custom_call_target="tpu_custom_call" | custom-call | tf_op jit(solution)/shard_map/pallas_call | solution.py:325
  72.9 1.0 %copy.18 = bf16[128,4096]{1,0:T(8,128)(2,1)} copy(bf16[128,4096]{1,0:T(8,128)(2,1)S(1)} %get-tuple-element.20) | data formatting | bytes 2097152
  73.8 0.8 %copy.19 = bf16[1,512,512]{2,1,0:T(8,128)(2,1)} copy(bf16[1,512,512]{2,1,0:T(8,128)(2,1)S(1)} %bitcast.5) | data formatting | bytes 1048576
  74.6 0.6 copy.20
  75.2 1.1 %copy.21 = f32[512,768]{1,0:T(8,128)} copy(f32[512,768]{1,0:T(8,128)S(1)} %get-tuple-element.23) | data formatting | bytes 3145728
  76.4 1.1 %copy.22 = f32[512,768]{1,0:T(8,128)} copy(f32[512,768]{1,0:T(8,128)S(1)} %get-tuple-element.24) | data formatting | bytes 3145728
Async XLA Ops:
  0.6 1.4 %copy-start = (f32[1,512,768]{2,1,0:T(8,128)S(1)}, f32[1,512,768]{2,1,0:T(8,128)}, u32[]{:S(2)}) copy-start(f32[1,512,768]{2,1,0:T(8,128)} %param.13) | copy-start | bytes 4718596
  2.0 1.4 %copy-start.1 = (f32[512,768]{1,0:T(8,128)S(1)}, f32[512,768]{1,0:T(8,128)}, u32[]{:S(2)}) copy-start(f32[512,768]{1,0:T(8,128)} %outer_h.1) | copy-start | bytes 4718596
  3.5 1.4 %copy-start.2 = (f32[512,768]{1,0:T(8,128)S(1)}, f32[512,768]{1,0:T(8,128)}, u32[]{:S(2)}) copy-start(f32[512,768]{1,0:T(8,128)} %mom_h.1) | copy-start | bytes 4718596
  4.9 1.2 %copy-start.3 = (bf16[128,4096]{1,0:T(8,128)(2,1)S(1)}, bf16[128,4096]{1,0:T(8,128)(2,1)}, u32[]{:S(2)}) copy-start(bf16[128,4096]{1,0:T(8,128)(2,1)} %hid.1) | copy-start | bytes 3145732
  6.1 1.2 %copy-start.4 = (bf16[128,4096]{1,0:T(8,128)(2,1)S(1)}, bf16[128,4096]{1,0:T(8,128)(2,1)}, u32[]{:S(2)}) copy-start(bf16[128,4096]{1,0:T(8,128)(2,1)} %res_h.1) | copy-start | bytes 3145732
  7.3 1.0 %copy-start.5 = (bf16[1,512,512]{2,1,0:T(8,128)(2,1)S(1)}, bf16[1,512,512]{2,1,0:T(8,128)(2,1)}, u32[]{:S(2)}) copy-start(bf16[1,512,512]{2,1,0:T(8,128)(2,1)} %param.11) | copy-start | bytes 1572868
  8.4 0.9 %copy-start.6 = (bf16[128,512]{1,0:T(8,128)(2,1)S(1)}, bf16[128,512]{1,0:T(8,128)(2,1)}, u32[]{:S(2)}) copy-start(bf16[128,512]{1,0:T(8,128)(2,1)} %vg.1) | copy-start | bytes 393220
  9.3 0.7 copy-start.7

commit v2 on v1

--- a/solution.py
+++ b/solution.py
@@ -15,10 +15,9 @@
 
 def kernel(
     n, reps, with_frag,
-    hid, res_h, vg, w, gain, inner_h, outer_h, mom_h,
-    hg_h, wg_out, gg_out, no_h, nm_h,
-    inv, nrm_s, nrm_r, vg_r, ig_s, ig_r, wg_acc, res, hg,
-    inner, outer, mom, ps, fr_r, av,
+    hid_h, res_h, vg_h, w_h, gain_h, inner_h, outer_h, mom_h,
+    hid, res, gain, inv, proj, ig_r, wg_out, gg_out, outer, mom,
+    nrm_s, nrm_r, vg_r, ig_s, wg_acc, w, inner, ps, fr_r, av,
     vg_send, vg_recv, nrm_send, nrm_recv, ig_send, ig_recv,
     fr_send, fr_recv, av_send, av_recv, local,
 ):
@@ -48,14 +47,17 @@
             device_id={axis: dest}, device_id_type=MESH,
         )
 
-    loads = [pltpu.make_async_copy(res_h, res, local.at[0])]
-    if with_frag:
-        loads += [
-            pltpu.make_async_copy(inner_h, inner, local.at[1]),
-            pltpu.make_async_copy(outer_h, outer, local.at[2]),
-            pltpu.make_async_copy(mom_h, mom, local.at[3]),
-        ]
-    for load in loads:
+    load_vg = pltpu.make_async_copy(vg_h, vg_r.at[me], local.at[0])
+    load_hid = pltpu.make_async_copy(hid_h, hid, local.at[1])
+    load_gain = pltpu.make_async_copy(gain_h, gain, local.at[2])
+    load_w = pltpu.make_async_copy(w_h, w, local.at[3])
+    load_res = pltpu.make_async_copy(res_h, res, local.at[4])
+    frag_loads = [
+        pltpu.make_async_copy(inner_h, inner, local.at[5]),
+        pltpu.make_async_copy(outer_h, outer, local.at[6]),
+        pltpu.make_async_copy(mom_h, mom, local.at[7]),
+    ] if with_frag else []
+    for load in [load_vg, load_hid, load_gain, load_w, *frag_loads, load_res]:
         load.start()
 
     barrier = pltpu.get_barrier_semaphore()
@@ -68,22 +70,29 @@
             pl.semaphore_signal(
                 barrier, inc=1, device_id={"replica": lax.rem(rep + k, reps)}, device_id_type=MESH
             )
+    load_vg.wait()
     pl.semaphore_wait(barrier, n - 1 + (reps - 1 if with_frag else 0))
 
     def vg_own(slot, dest):
-        return remote(vg, vg_r.at[me], vg_send.at[slot], vg_recv.at[me], dest)
+        return remote(vg_r.at[me], vg_r.at[me], vg_send.at[slot], vg_recv.at[me], dest)
 
     def vg_forward(j):
         return remote(
             vg_r.at[mirror], vg_r.at[mirror], vg_send.at[half + j], vg_recv.at[mirror], near_peer(j)
         )
 
+    def vg_wait(src):
+        remote(
+            vg_r.at[src], vg_r.at[src], vg_send.at[0], vg_recv.at[src], mirror
+        ).wait_recv()
+
     vg_own(0, mirror).start()
     for j in range(1, half):
         vg_own(j, near_peer(j)).start()
-    vg_r[me] = vg[...]
 
     rows = 16
+    tall = 32
+    load_hid.wait()
 
     @pl.loop(0, tokens // rows)
     def _(c):
@@ -95,12 +104,14 @@
         mean = jnp.sum(total, axis=1, keepdims=True) / width
         inv[at, :] = jnp.broadcast_to(lax.rsqrt(mean + EPS), (rows, 128))
 
+    load_gain.wait()
+
     def norm_block(dest, out, slot):
         scale = gain[:, cols(dest)]
 
-        @pl.loop(0, tokens // rows)
+        @pl.loop(0, tokens // tall)
         def _(c):
-            at = pl.ds(pl.multiple_of(c * rows, rows), rows)
+            at = pl.ds(pl.multiple_of(c * tall, tall), tall)
             unit = hid[at, cols(dest)].astype(F32) * inv[at, 0:1]
             out[slot, at, :] = (unit * scale).astype(BF16)
 
@@ -138,7 +149,7 @@
     if with_frag:
         share = ps.shape[1]
         steps = share // rows
-        for load in loads[1:]:
+        for load in frag_loads:
             load.wait()
 
         @pl.loop(0, reps * steps)
@@ -150,9 +161,11 @@
         for k in range(1, reps):
             fr_copy(k).start()
 
-    remote(vg, vg_r.at[mirror], vg_send.at[0], vg_recv.at[mirror], mirror).wait_recv()
+    vg_wait(mirror)
     for j in range(1, half):
         vg_forward(j).start()
+
+    load_w.wait()
 
     def ig_dot(src):
         return lax.dot_general(
@@ -162,9 +175,6 @@
     def ig_copy(src):
         return remote(ig_s.at[src], ig_r.at[me], ig_send.at[src], ig_recv.at[me], src)
 
-    def vg_wait(src):
-        remote(vg, vg_r.at[src], vg_send.at[0], vg_recv.at[src], src).wait_recv()
-
     ig_s[mirror] = ig_dot(mirror)
     ig_copy(mirror).start()
 
@@ -186,7 +196,6 @@
     ig_s[me] = own
     ig_r[me] = own
 
-    stores = []
     if with_frag:
         for k in range(1, reps):
             src = lax.rem(rep + k, reps)
@@ -220,42 +229,6 @@
             mom[at, :] = momentum
             outer[at, :] = outer[at, :] - 0.7 * (average + 0.9 * momentum)
 
-        stores += [
-            pltpu.make_async_copy(outer, no_h, local.at[1]),
-            pltpu.make_async_copy(mom, nm_h, local.at[2]),
-        ]
-        for store in stores:
-            store.start()
-
-    loads[0].wait()
-
-    @pl.loop(1, n)
-    def _(k):
-        src = lax.rem(me + k, n)
-        remote(ig_s.at[src], ig_r.at[src], ig_send.at[src], ig_recv.at[src], src).wait_recv()
-
-    @pl.loop(0, tokens // rows)
-    def _(c):
-        at = pl.ds(pl.multiple_of(c * rows, rows), rows)
-        inverse = inv[at, 0:1]
-        total = jnp.zeros((rows, feats), F32)
-        for b in range(n):
-            span = slice(b * feats, (b + 1) * feats)
-            unit = hid[at, span].astype(F32) * inverse
-            total += (ig_r[b, at, :].astype(F32) * gain[:, span]) * unit
-        projection = jnp.sum(total, axis=1, keepdims=True) / width
-        for b in range(n):
-            span = slice(b * feats, (b + 1) * feats)
-            unit = hid[at, span].astype(F32) * inverse
-            scaled = ig_r[b, at, :].astype(F32) * gain[:, span]
-            hg[at, span] = (
-                res[at, span].astype(F32) + inverse * (scaled - unit * projection)
-            ).astype(BF16)
-
-    store = pltpu.make_async_copy(hg, hg_h, local.at[0])
-    store.start()
-    stores.append(store)
-
     def wg_dot(src):
         return lax.dot_general(
             nrm_r[src], vg_r[src], (((0,), (0,)), ((), ())), preferred_element_type=F32
@@ -267,17 +240,50 @@
     wg_acc[...] = wg_dot(me)
     gg_out[...] = gg_sum(me)
 
-    @pl.loop(1, n)
-    def _(k):
-        src = lax.rem(me + k, n)
+    def add_group(src):
         remote(
             nrm_s.at[src], nrm_r.at[src], nrm_send.at[src], nrm_recv.at[src], src
         ).wait_recv()
         wg_acc[...] += wg_dot(src)
         gg_out[...] += gg_sum(src)
 
+    @pl.loop(1, half)
+    def _(j):
+        add_group(near_peer(j))
+
+    @pl.loop(0, half)
+    def _(j):
+        add_group(far_peer(j))
+
     wg_out[...] = wg_acc[...].astype(BF16)
     gg_out[...] = gg_out[...] / gain[:, cols(me)]
+
+    def project(src, first):
+        scale = gain[:, cols(src)]
+
+        @pl.loop(0, tokens // tall)
+        def _(c):
+            at = pl.ds(pl.multiple_of(c * tall, tall), tall)
+            unit = hid[at, cols(src)].astype(F32) * inv[at, 0:1]
+            term = (ig_r[src, at, :].astype(F32) * scale) * unit
+            total = term[:, :128]
+            for g in range(1, feats // 128):
+                total += term[:, g * 128:(g + 1) * 128]
+            proj[at, :] = total if first else proj[at, :] + total
+
+    def add_block(src):
+        remote(ig_s.at[src], ig_r.at[src], ig_send.at[src], ig_recv.at[src], src).wait_recv()
+        project(src, False)
+
+    project(me, True)
+
+    @pl.loop(1, half)
+    def _(j):
+        add_block(near_peer(j))
+
+    @pl.loop(0, half)
+    def _(j):
+        add_block(far_peer(j))
 
     vg_own(0, mirror).wait_send()
     for j in range(1, half):
@@ -290,6 +296,43 @@
         for k in range(1, reps):
             fr_copy(k).wait_send()
             av_copy(k).wait_send()
+    load_res.wait()
+
+
+def finish(
+    n, with_frag,
+    hid, res, gain, inv, proj, ig, wg, gg, outer, mom,
+    hg_h, wg_h, gg_h, no_h, nm_h,
+    hg, sems, hg_sems,
+):
+    tokens, width = hid.shape
+    feats = width // n
+    tall = 32
+    pairs = [(wg, wg_h), (gg, gg_h)] + ([(outer, no_h), (mom, nm_h)] if with_frag else [])
+    stores = [pltpu.make_async_copy(a, b, sems.at[i]) for i, (a, b) in enumerate(pairs)]
+    for store in stores:
+        store.start()
+
+    def hg_store(c):
+        at = pl.ds(pl.multiple_of(c * tall, tall), tall)
+        return pltpu.make_async_copy(hg.at[at], hg_h.at[at], hg_sems.at[c])
+
+    @pl.loop(0, tokens // tall)
+    def _(c):
+        at = pl.ds(pl.multiple_of(c * tall, tall), tall)
+        inverse = inv[at, 0:1]
+        projection = jnp.sum(proj[at, :], axis=1, keepdims=True) / width
+        for b in range(n):
+            span = slice(b * feats, (b + 1) * feats)
+            unit = hid[at, span].astype(F32) * inverse
+            scaled = ig[b, at, :].astype(F32) * gain[:, span]
+            hg[at, span] = (
+                res[at, span].astype(F32) + inverse * (scaled - unit * projection)
+            ).astype(BF16)
+        hg_store(c).start()
+
+    for c in range(tokens // tall):
+        hg_store(c).wait()
     for store in stores:
         store.wait()
 
@@ -319,46 +362,63 @@
     half_buffer = (slots, share, frag_cols) if with_frag else (1, 16, 128)
 
     vmem = pl.BlockSpec(memory_space=pltpu.VMEM)
-    anywhere = pl.BlockSpec(memory_space=pl.ANY)
-    frag_out = frag_buffer
+    hbm = pl.BlockSpec(memory_space=pltpu.HBM)
     dma = pltpu.SemaphoreType.DMA
-    hidden_grad, weight_grad, gain_grad, new_outer, new_momentum = pl.pallas_call(
+    in_hbm = [
+        pltpu.with_memory_space_constraint(x, pltpu.HBM)
+        for x in (
+            hidden_in, res_grad, value_grad, value_weight[0], norm_gain,
+            inner_frag[0], outer_frag, momentum,
+        )
+    ]
+    held = pl.pallas_call(
         functools.partial(kernel, n, reps, with_frag),
         out_shape=(
             jax.ShapeDtypeStruct((tokens, width), BF16),
+            jax.ShapeDtypeStruct((tokens, width), BF16),
+            jax.ShapeDtypeStruct((1, width), F32),
+            jax.ShapeDtypeStruct((tokens, 128), F32),
+            jax.ShapeDtypeStruct((tokens, 128), F32),
+            jax.ShapeDtypeStruct((n, tokens, feats), BF16),
             jax.ShapeDtypeStruct((feats, values), BF16),
             jax.ShapeDtypeStruct((1, feats), F32),
-            jax.ShapeDtypeStruct(frag_out, F32),
-            jax.ShapeDtypeStruct(frag_out, F32),
+            jax.ShapeDtypeStruct(frag_buffer, F32),
+            jax.ShapeDtypeStruct(frag_buffer, F32),
         ),
-        in_specs=[vmem, anywhere, vmem, vmem, vmem, anywhere, anywhere, anywhere],
-        out_specs=(anywhere, vmem, vmem, anywhere, anywhere),
+        in_specs=[hbm] * 8,
+        out_specs=(vmem,) * 10,
         scratch_shapes=[
-            pltpu.VMEM((tokens, 128), F32),
             pltpu.VMEM((n, tokens, feats), BF16),
             pltpu.VMEM((n, tokens, feats), BF16),
             pltpu.VMEM((n, tokens, values), BF16),
             pltpu.VMEM((n, tokens, feats), BF16),
-            pltpu.VMEM((n, tokens, feats), BF16),
             pltpu.VMEM((feats, values), F32),
-            pltpu.VMEM((tokens, width), BF16),
-            pltpu.VMEM((tokens, width), BF16),
-            pltpu.VMEM(frag_buffer, F32),
-            pltpu.VMEM(frag_buffer, F32),
+            pltpu.VMEM((feats, values), BF16),
             pltpu.VMEM(frag_buffer, F32),
             pltpu.VMEM(half_buffer, BF16),
             pltpu.VMEM(half_buffer, BF16),
             pltpu.VMEM(half_buffer, BF16),
             dma((n,)), dma((n,)), dma((n,)), dma((n,)), dma((n,)), dma((n,)),
-            dma((slots,)), dma((slots,)), dma((slots,)), dma((slots,)), dma((4,)),
+            dma((slots,)), dma((slots,)), dma((slots,)), dma((slots,)), dma((8,)),
         ],
         compiler_params=pltpu.CompilerParams(
-            collective_id=0, has_side_effects=True, vmem_limit_bytes=40 * 2**20
+            collective_id=0, has_side_effects=True, vmem_limit_bytes=32 * 2**20
         ),
-    )(
-        hidden_in, res_grad, value_grad, value_weight[0], norm_gain,
-        inner_frag[0], outer_frag, momentum,
-    )
+    )(*in_hbm)
+    hidden_grad, weight_grad, gain_grad, new_outer, new_momentum = pl.pallas_call(
+        functools.partial(finish, n, with_frag),
+        out_shape=(
+            jax.ShapeDtypeStruct((tokens, width), BF16),
+            jax.ShapeDtypeStruct((feats, values), BF16),
+            jax.ShapeDtypeStruct((1, feats), F32),
+            jax.ShapeDtypeStruct(frag_buffer, F32),
+            jax.ShapeDtypeStruct(frag_buffer, F32),
+        ),
+        in_specs=[vmem] * 10,
+        out_specs=(hbm,) * 5,
+        scratch_shapes=[pltpu.VMEM((tokens, width), BF16), dma((4,)), dma((tokens // 32,))],
+        compiler_params=pltpu.CompilerParams(vmem_limit_bytes=32 * 2**20),
+    )(*held)
     if not with_frag:
         new_outer, new_momentum = outer_step(inner_frag[0], outer_frag, momentum)
     return (hidden_grad, weight_grad[None], gain_grad, new_outer, new_momentum)

time: 78.3 us -> 62.6 us (0.80)
  local copies, waits for them, and re-layouts: 14 us -> 0 us
  Pallas kernels: 62.9 us -> 61.4 us
    unnamed x21 -> x0, local copies, waits for them, and re-layouts: 14 us -> none
    pallas_call x1, Pallas kernels: 62.9 us -> 59.1 us  [body(): pl.pallas_call(functools.partial(kernel, n, reps, with_frag), out_shape=(...]
    pallas_call x0 -> x1, Pallas kernels: none -> 2.25 us  [body(): pl.pallas_call(functools.partial(finish, n, with_frag), out_shape=(jax.Sh...]
where the time goes in v2:
time: 62.6 us; the launch traced here: 62 us
  Pallas kernels  61.4 us (98%)
  between operations  0.64 us (1%)
    pallas_call x1, Pallas kernels, body(): pl.pallas_call(functools.partial(kernel, n, reps, with_frag), out_shape=(...  59.1 us
    pallas_call x1, Pallas kernels, body(): pl.pallas_call(functools.partial(finish, n, with_frag), out_shape=(jax.Sh...  2.25 us

profile of v2, /device:TPU:0, one launch (start us, length us, event | category | flops | bytes accessed | tf_op | source)
XLA Modules:
  0.0 62.0 jit_solution(18105912955922577964)
XLA Ops:
  0.6 59.1 %shard_map.119 = (bf16[128,4096]{1,0:T(8,128)(2,1)S(1)}, bf16[128,4096]{1,0:T(8,128)(2,1)S(1)}, f32[1,4096]{1,0:T(1,128)S(1)}, f32[128,128]{1,0:T(8,128)S(1)}, f...) custom-call(bf16[128,4096]{1,0:T(8,128)(2,1)} %hid_h.1, ...), custom_call_target="tpu_custom_call" | custom-call | tf_op jit(solution)/shard_map/pallas_call | solution.py:374
  59.8 2.2 %shard_map.120 = (bf16[128,4096]{1,0:T(8,128)(2,1)}, bf16[512,512]{1,0:T(8,128)(2,1)}, f32[1,512]{1,0:T(1,128)}, f32[512,768]{1,0:T(8,128)}, f32[512,768]{1,0:T(8,128)}) custom-call(bf16[128,4096]{1,0:T(8,128)(2,1)S(1)} %get-tuple-element.20.hid, bf16[128,4096]{1,0:T(8,128)(2,1)S(1)} %get-tuple-element.21.res, f32[1,4096]{1,0:T(1,128)S(1)} %get-tuple-element.22.gain, ...), custom_call_target="tpu_custom_call" | custom-call | tf_op jit(solution)/shard_map/pallas_call | solution.py:408

commit v3 on v2

--- a/solution.py
+++ b/solution.py
@@ -38,6 +38,12 @@
     def far_peer(j):
         return far + lax.rem(theirs + j, half)
 
+    def near_source(j):
+        return base + lax.rem(mine + half - j, half)
+
+    def far_source(j):
+        return far + lax.rem(theirs + half - j, half)
+
     def cols(i):
         return pl.ds(pl.multiple_of(i * feats, feats), feats)
 
@@ -180,14 +186,14 @@
 
     @pl.loop(1, half)
     def _(j):
-        src = near_peer(j)
+        src = near_source(j)
         vg_wait(src)
         ig_s[src] = ig_dot(src)
         ig_copy(src).start()
 
     @pl.loop(1, half)
     def _(j):
-        src = far_peer(j)
+        src = far_source(j)
         vg_wait(src)
         ig_s[src] = ig_dot(src)
         ig_copy(src).start()
@@ -237,26 +243,12 @@
     def gg_sum(src):
         return jnp.sum(nrm_r[src].astype(F32) * ig_s[src].astype(F32), axis=0, keepdims=True)
 
-    wg_acc[...] = wg_dot(me)
-    gg_out[...] = gg_sum(me)
-
     def add_group(src):
         remote(
             nrm_s.at[src], nrm_r.at[src], nrm_send.at[src], nrm_recv.at[src], src
         ).wait_recv()
         wg_acc[...] += wg_dot(src)
         gg_out[...] += gg_sum(src)
-
-    @pl.loop(1, half)
-    def _(j):
-        add_group(near_peer(j))
-
-    @pl.loop(0, half)
-    def _(j):
-        add_group(far_peer(j))
-
-    wg_out[...] = wg_acc[...].astype(BF16)
-    gg_out[...] = gg_out[...] / gain[:, cols(me)]
 
     def project(src, first):
         scale = gain[:, cols(src)]
@@ -275,15 +267,22 @@
         remote(ig_s.at[src], ig_r.at[src], ig_send.at[src], ig_recv.at[src], src).wait_recv()
         project(src, False)
 
+    wg_acc[...] = wg_dot(me)
+    gg_out[...] = gg_sum(me)
     project(me, True)
 
     @pl.loop(1, half)
     def _(j):
+        add_group(near_source(j))
         add_block(near_peer(j))
 
     @pl.loop(0, half)
     def _(j):
+        add_group(far_source(j))
         add_block(far_peer(j))
+
+    wg_out[...] = wg_acc[...].astype(BF16)
+    gg_out[...] = gg_out[...] / gain[:, cols(me)]
 
     vg_own(0, mirror).wait_send()
     for j in range(1, half):

time: 62.6 us -> 62.8 us (level)
  no operation moved by 1% of the time
where the time goes in v3:
time: 62.8 us; the launch traced here: 62.6 us
  Pallas kernels  62 us (99%)
  between operations  0.64 us (1%)
    pallas_call x1, Pallas kernels, body(): pl.pallas_call(functools.partial(kernel, n, reps, with_frag), out_shape=(...  59.7 us
    pallas_call x1, Pallas kernels, body(): pl.pallas_call(functools.partial(finish, n, with_frag), out_shape=(jax.Sh...  2.25 us

profile of v3, /device:TPU:0, one launch (start us, length us, event | category | flops | bytes accessed | tf_op | source)
XLA Modules:
  0.0 62.6 jit_solution(3563378189402148523)
XLA Ops:
  0.6 59.7 %shard_map.119 = (bf16[128,4096]{1,0:T(8,128)(2,1)S(1)}, bf16[128,4096]{1,0:T(8,128)(2,1)S(1)}, f32[1,4096]{1,0:T(1,128)S(1)}, f32[128,128]{1,0:T(8,128)S(1)}, f...) custom-call(bf16[128,4096]{1,0:T(8,128)(2,1)} %hid_h.1, ...), custom_call_target="tpu_custom_call" | custom-call | tf_op jit(solution)/shard_map/pallas_call | solution.py:373
  60.4 2.2 %shard_map.120 = (bf16[128,4096]{1,0:T(8,128)(2,1)}, bf16[512,512]{1,0:T(8,128)(2,1)}, f32[1,512]{1,0:T(1,128)}, f32[512,768]{1,0:T(8,128)}, f32[512,768]{1,0:T(8,128)}) custom-call(bf16[128,4096]{1,0:T(8,128)(2,1)S(1)} %get-tuple-element.20.hid, bf16[128,4096]{1,0:T(8,128)(2,1)S(1)} %get-tuple-element.21.res, f32[1,4096]{1,0:T(1,128)S(1)} %get-tuple-element.22.gain, ...), custom_call_target="tpu_custom_call" | custom-call | tf_op jit(solution)/shard_map/pallas_call | solution.py:407

commit v4 on v3

--- a/solution.py
+++ b/solution.py
@@ -126,17 +126,16 @@
             nrm_s.at[dest], nrm_r.at[me], nrm_send.at[dest], nrm_recv.at[me], dest
         )
 
-    @pl.loop(0, half)
-    def _(j):
-        dest = far_peer(j)
+    def send_normed(dest):
         norm_block(dest, nrm_s, dest)
         nrm_copy(dest).start()
 
+    send_normed(mirror)
+
     @pl.loop(1, half)
     def _(j):
-        dest = near_peer(j)
-        norm_block(dest, nrm_s, dest)
-        nrm_copy(dest).start()
+        send_normed(near_peer(j))
+        send_normed(far_peer(j))
 
     norm_block(me, nrm_r, me)
 
@@ -184,19 +183,15 @@
     ig_s[mirror] = ig_dot(mirror)
     ig_copy(mirror).start()
 
-    @pl.loop(1, half)
-    def _(j):
-        src = near_source(j)
+    def send_block(src):
         vg_wait(src)
         ig_s[src] = ig_dot(src)
         ig_copy(src).start()
 
     @pl.loop(1, half)
     def _(j):
-        src = far_source(j)
-        vg_wait(src)
-        ig_s[src] = ig_dot(src)
-        ig_copy(src).start()
+        send_block(near_source(j))
+        send_block(far_source(j))
 
     own = ig_dot(me)
     ig_s[me] = own

time: 62.8 us -> 62.3 us (level)
  no operation moved by 1% of the time
where the time goes in v4:
time: 62.3 us; the launch traced here: 62.2 us
  Pallas kernels  61.5 us (99%)
  between operations  0.64 us (1%)
    pallas_call x1, Pallas kernels, body(): pl.pallas_call(functools.partial(kernel, n, reps, with_frag), out_shape=(...  59.3 us
    pallas_call x1, Pallas kernels, body(): pl.pallas_call(functools.partial(finish, n, with_frag), out_shape=(jax.Sh...  2.25 us

profile of v4, /device:TPU:0, one launch (start us, length us, event | category | flops | bytes accessed | tf_op | source)
XLA Modules:
  0.0 62.2 jit_solution(14687638556382668315)
XLA Ops:
  0.6 59.3 %shard_map.119 = (bf16[128,4096]{1,0:T(8,128)(2,1)S(1)}, bf16[128,4096]{1,0:T(8,128)(2,1)S(1)}, f32[1,4096]{1,0:T(1,128)S(1)}, f32[128,128]{1,0:T(8,128)S(1)}, f...) custom-call(bf16[128,4096]{1,0:T(8,128)(2,1)} %hid_h.1, ...), custom_call_target="tpu_custom_call" | custom-call | tf_op jit(solution)/shard_map/pallas_call | solution.py:368
  59.9 2.2 %shard_map.120 = (bf16[128,4096]{1,0:T(8,128)(2,1)}, bf16[512,512]{1,0:T(8,128)(2,1)}, f32[1,512]{1,0:T(1,128)}, f32[512,768]{1,0:T(8,128)}, f32[512,768]{1,0:T(8,128)}) custom-call(bf16[128,4096]{1,0:T(8,128)(2,1)S(1)} %get-tuple-element.20.hid, bf16[128,4096]{1,0:T(8,128)(2,1)S(1)} %get-tuple-element.21.res, f32[1,4096]{1,0:T(1,128)S(1)} %get-tuple-element.22.gain, ...), custom_call_target="tpu_custom_call" | custom-call | tf_op jit(solution)/shard_map/pallas_call | solution.py:402
